TPU v7x, 128 devices: a whole 4x4x4 slice. The times are simulated.
128 devices in a mesh: node: 32 (over y, x, z_lo), local: 4 (over z_hi, core).
Axes of the slice: x: 4, y: 4, z: 4 (z_hi: 2, z_lo: 2; z = z_hi * 2 + z_lo), core: 2. Of those that a mesh axis runs over, the one named last changes fastest.
Arguments:
- tokens: bfloat16 [16384, 4096], P(('node', 'local')), may hold values from -6 to 6
- grad_out: bfloat16 [16384, 4096], P(('node', 'local')), may hold values from -6 to 6
- router_logits: float32 [16384, 128], P(('node', 'local')), may hold values from -20 to 280
- group_id: int32 [16384], P(('node', 'local')), may hold values from 0 to 15, as said below
- expert_ids: int32 [16384, 2], P(('node', 'local')), may hold values from 0 to 7, as said below
- w_gate: bfloat16 [32, 4096, 1536], P('node', None, 'local'), may hold values from -0.09375 to 0.09375
- w_up: bfloat16 [32, 4096, 1536], P('node', None, 'local'), may hold values from -0.09375 to 0.09375
- w_down: bfloat16 [32, 1536, 4096], P('node', 'local'), may hold values from -0.15625 to 0.15625
Outputs:
- mixed: bfloat16 [16384, 4096], P(('node', 'local'))
- d_tokens: bfloat16 [16384, 4096], P(('node', 'local'))
- d_logits: float32 [16384, 128], P(('node', 'local'))
- grad_gate: bfloat16 [32, 4096, 1536], P('node', None, 'local')
- grad_up: bfloat16 [32, 4096, 1536], P('node', None, 'local')
- grad_down: bfloat16 [32, 1536, 4096], P('node', 'local')
Inputs may be any that keep to these rules, and one draw needn't show every extreme that they name: `group_id`: A token is computed here when its group is below 4. Among the tokens of one device no expert of those groups is named by more than 6 tokens, and one such expert is named by exactly 6 tokens of every device. `expert_ids`: the two numbers of a token differ; both name experts of the token's group.
All inputs are finite; a program needn't handle non-finite values.
Results may differ from a plain program's by a relative error of at most 0.0065.
Values may be sent and summed in bfloat16 or wider, within the bound.
No kernel may reach another device: no remote copies, remote signals or barrier semaphores. Data moves between devices by JAX's collectives and lax.ppermute only.
A program may use at most 192 MiB of HBM per device.

v0:
```python
import jax
import jax.numpy as jnp
from jax import lax
from jax.sharding import PartitionSpec as P

GSIZE = 8
CAP = 6


def cut_along(value, dim, length):
    lengths = value.shape
    pieces = value.reshape(*lengths[:dim], length, lengths[dim] // length, *lengths[dim + 1 :])
    return jnp.moveaxis(pieces, dim, 0)


def piece_ends(length, count):
    unit = 8 if length >= 8 * count else 1
    return [length // unit * k // count * unit for k in range(1, count)]


def in_order(pieces, dim):
    pieces = jnp.moveaxis(pieces, 0, dim)
    lengths = pieces.shape
    return pieces.reshape(*lengths[:dim], lengths[dim] * lengths[dim + 1], *lengths[dim + 2 :])


def exchange_in_pieces(value, axis, pieces, split_dim, concat_dim):
    blocks = cut_along(value, split_dim, lax.axis_size(axis))
    cut = max(range(1, max(2, blocks.ndim - 1)), key=lambda d: blocks.shape[d])
    outs = []
    for piece in jnp.split(blocks, piece_ends(blocks.shape[cut], pieces), axis=cut):
        if piece.size:
            outs.append(lax.all_to_all(piece, axis, split_axis=0, concat_axis=0, tiled=True))
    return in_order(jnp.concatenate(outs, axis=cut), concat_dim)


def gate_weights(logits, group_ids, chosen, inside):
    probabilities = jax.nn.softmax(logits, axis=-1)
    columns = jnp.arange(logits.shape[1], dtype=jnp.int32)
    member = ((columns // GSIZE)[None, :] == group_ids[:, None]).astype(logits.dtype)
    group_mass = jnp.sum(probabilities * member, axis=1)
    picked = jnp.sum(
        jnp.where(chosen[:, :, None] == columns[None, None, :], logits[:, None, :], 0.0), axis=2
    )
    pair_share = jax.nn.softmax(picked, axis=-1)
    return jnp.where(inside[:, None], group_mass[:, None] * pair_share, 0.0)


def spread(buffer):
    arrived = lax.all_to_all(buffer, "node", split_axis=0, concat_axis=2, tiled=True)
    arrived = lax.all_gather(arrived, "local", axis=2, tiled=True)
    return arrived[0]


def collect(partial_sums):
    summed = lax.psum_scatter(partial_sums[None], "local", scatter_dimension=2, tiled=True)
    result = exchange_in_pieces(summed.astype(jnp.bfloat16), "node", 2, 2, 0)
    return result.reshape(-1, result.shape[-1])


def body(tokens, grad_out, router_logits, group_id, expert_ids, w_gate, w_up, w_down):
    owned_count = w_gate.shape[0]
    node_count = lax.axis_size("node")
    expert_total = owned_count * node_count
    window_groups = expert_total // GSIZE
    model_width = tokens.shape[1]
    inside = group_id < window_groups
    chosen = group_id[:, None] * GSIZE + expert_ids
    target = jnp.where(inside[:, None], chosen, expert_total)
    expert_range = jnp.arange(expert_total, dtype=jnp.int32)
    onehot = (target[:, :, None] == expert_range[None, None, :]).astype(jnp.int32)
    per_token = jnp.sum(onehot, axis=1)
    earlier = jnp.cumsum(per_token, axis=0) - per_token
    slot_rank = jnp.sum(onehot * earlier[:, None, :], axis=2)
    slot_index = jnp.where(inside[:, None], target * CAP + slot_rank, -1)
    slot_range = jnp.arange(expert_total * CAP, dtype=jnp.int32)
    first_pick = (slot_range[:, None] == slot_index[None, :, 0]).astype(jnp.bfloat16)
    second_pick = (slot_range[:, None] == slot_index[None, :, 1]).astype(jnp.bfloat16)
    mix_weights, pull_back = jax.vjp(
        lambda values: gate_weights(values, group_id, chosen, inside), router_logits
    )
    grad_f32 = grad_out.astype(jnp.float32)
    first_grad = (mix_weights[:, 0:1] * grad_f32).astype(jnp.bfloat16)
    second_grad = (mix_weights[:, 1:2] * grad_f32).astype(jnp.bfloat16)
    send_rows = (
        jnp.dot(first_pick, tokens, preferred_element_type=jnp.float32)
        + jnp.dot(second_pick, tokens, preferred_element_type=jnp.float32)
    ).astype(jnp.bfloat16)
    send_grads = (
        jnp.dot(first_pick, first_grad, preferred_element_type=jnp.float32)
        + jnp.dot(second_pick, second_grad, preferred_element_type=jnp.float32)
    ).astype(jnp.bfloat16)
    buffer_shape = (node_count, owned_count, CAP, model_width)
    rows_in = spread(send_rows.reshape(buffer_shape))
    gate_pre = jnp.einsum("erd,edf->erf", rows_in, w_gate, preferred_element_type=jnp.float32)
    up_pre = jnp.einsum("erd,edf->erf", rows_in, w_up, preferred_element_type=jnp.float32)
    sigmoid_gate = jax.nn.sigmoid(gate_pre)
    activated = gate_pre * sigmoid_gate
    hidden = (activated * up_pre).astype(jnp.bfloat16)
    partial_out = jnp.einsum("erf,efd->erd", hidden, w_down, preferred_element_type=jnp.float32)
    out_flat = collect(partial_out)
    grads_in = spread(send_grads.reshape(buffer_shape))
    grad_hidden = jnp.einsum("erd,efd->erf", grads_in, w_down, preferred_element_type=jnp.float32)
    grad_gate_pre = (
        grad_hidden * up_pre * sigmoid_gate * (1.0 + gate_pre * (1.0 - sigmoid_gate))
    ).astype(jnp.bfloat16)
    grad_up_pre = (grad_hidden * activated).astype(jnp.bfloat16)
    partial_in = jnp.einsum(
        "erf,edf->erd", grad_gate_pre, w_gate, preferred_element_type=jnp.float32
    ) + jnp.einsum("erf,edf->erd", grad_up_pre, w_up, preferred_element_type=jnp.float32)
    back_flat = collect(partial_in)
    grad_gate = jnp.einsum(
        "erd,erf->edf", rows_in, grad_gate_pre, preferred_element_type=jnp.float32
    ).astype(jnp.bfloat16)
    grad_up = jnp.einsum(
        "erd,erf->edf", rows_in, grad_up_pre, preferred_element_type=jnp.float32
    ).astype(jnp.bfloat16)
    grad_down = jnp.einsum(
        "erf,erd->efd", hidden, grads_in, preferred_element_type=jnp.float32
    ).astype(jnp.bfloat16)
    first_out = jnp.einsum("st,sd->td", first_pick, out_flat, preferred_element_type=jnp.float32)
    second_out = jnp.einsum("st,sd->td", second_pick, out_flat, preferred_element_type=jnp.float32)
    first_back = jnp.einsum("st,sd->td", first_pick, back_flat, preferred_element_type=jnp.float32)
    second_back = jnp.einsum(
        "st,sd->td", second_pick, back_flat, preferred_element_type=jnp.float32
    )
    mixed = (mix_weights[:, 0:1] * first_out + mix_weights[:, 1:2] * second_out).astype(
        jnp.bfloat16
    )
    d_tokens = (first_back + second_back).astype(jnp.bfloat16)
    scores = jnp.stack(
        [jnp.sum(grad_f32 * first_out, axis=1), jnp.sum(grad_f32 * second_out, axis=1)], axis=1
    )
    d_logits = pull_back(scores)[0]
    return (mixed, d_tokens, d_logits, grad_gate, grad_up, grad_down)


def solution(mesh):
    return jax.shard_map(
        body,
        mesh=mesh,
        in_specs=(
            P(("node", "local"), None),
            P(("node", "local"), None),
            P(("node", "local"), None),
            P(("node", "local")),
            P(("node", "local"), None),
            P("node", None, "local"),
            P("node", None, "local"),
            P("node", "local", None),
        ),
        out_specs=(
            P(("node", "local"), None),
            P(("node", "local"), None),
            P(("node", "local"), None),
            P("node", None, "local"),
            P("node", None, "local"),
            P("node", "local", None),
        ),
        check_vma=False,
    )
```

profile of v0, /device:TPU:0, one launch (start us, length us, event | category | flops | bytes accessed | tf_op | source)
XLA Modules:
  0.0 582.0 jit_solution(17738413348024515923)
XLA Ops:
  7.2 0.8 broadcast_compare_fusion
  8.0 0.8 broadcast_multiply_fusion
  8.8 0.7 broadcast_select_fusion
  9.5 0.1 copy.29
  9.6 0.2 reduce_window_sum.11
  9.8 0.1 copy.31
  9.9 1.9 fusion.53
  11.8 1.7 fusion.30
  13.5 3.5 reshape.156
  17.0 37.9 %all_to_all.44 = bf16[32,1,6,4096]{3,2,1,0:T(8,128)(2,1)} all-to-all(bf16[32,1,6,4096]{3,2,1,0:T(8,128)(2,1)} %bitcast.95), channel_id=1, replica_groups=mesh['node'=32,'local'=4] {'node'}, dimensions={0} | all-to-all | bytes 3145728 | tf_op jit(solution)/shard_map/all_to_all | solution.py:50
  54.9 3.7 all_to_all.31
  58.6 0.0 reduce-scatter.3.cloned.1.call-start
  58.7 48.7 %all-gather.3.cloned.1.call-done = bf16[1,1,768,4096]{3,2,1,0:T(8,128)(2,1)} async-done(((bf16[1,1,192,4096]{3,2,1,0:T(8,128)(2,1)}), bf16[1,1,768,4096]{3,2,1,0:T(8,128)(2,1)}) %all-gather.3.cloned.1.call-update) | async-done | bytes 6291472 | tf_op jit(solution)/shard_map/all_gather | solution.py:51
  107.4 6.6 %fusion.10 = f32[768,384]{1,0:T(8,128)S(1)} fusion(bf16[1,1,768,4096]{3,2,1,0:T(8,128)(2,1)} %all-gather.3.cloned.1.call-done, bf16[1,4096,384]{2,1,0:T(8,128)(2,1)} %param.13), kind=kOutput, calls=%fused_computation.12 | convolution fusion | flops 2415919104 | bytes 10616832 | tf_op jit(solution)/shard_map/erd,edf->erf/dot_general | solution.py:95
  114.0 4.5 multiply_convert_fusion.2
  118.5 0.8 copy-done.8
  119.3 6.4 %convolution_bitcast_fusion = f32[1,1,768,4096]{3,2,1,0:T(8,128)} fusion(bf16[768,384]{1,0:T(8,128)(2,1)S(1)} %get-tuple-element.26, bf16[1,384,4096]{2,1,0:T(8,128)(2,1)S(1)} %copy-done), kind=kOutput, calls=%fused_computation.1 | convolution fusion | flops 2415919104 | bytes 16318464 | tf_op jit(solution)/shard_map/erf,efd->erd/dot_general | solution.py:100
  125.8 105.4 %reduce-scatter.3.cloned.1.call-done = f32[1,1,192,4096]{3,2,1,0:T(8,128)} async-done(((f32[1,1,768,4096]{3,2,1,0:T(8,128)}), f32[1,1,192,4096]{3,2,1,0:T(8,128)}) %reduce-scatter.3.cloned.1.call-update) | async-done | bytes 3145744 | tf_op jit(solution)/shard_map/reduce_scatter | solution.py:56
  231.2 3.2 convert_element_type.66
  234.4 3.5 transpose_reshape.6
  237.9 4.7 slice_bitcast_fusion.3
  242.6 7.4 %all-to-all-start.1 = ((bf16[32,1,1,3,4096]{4,3,2,1,0:T(4,128)(2,1)}), bf16[32,1,1,3,4096]{4,3,2,1,0:T(4,128)(2,1)}, u32[]{:S(2)}, u32[]{:S(2)}) async-start(bf16[32,1,1,3,4096]{4,3,2,1,0:T(4,128)(2,1)} %get-tuple-element.18), calls=%async_computation.2 | async-start | bytes 2097152 | tf_op jit(solution)/shard_map/all_to_all | solution.py:33
  250.1 0.1 reduce_max.18
  250.2 0.2 select_reduce_fusion.1
  250.4 17.5 %all-to-all-done.1 = bf16[32,1,1,3,4096]{4,3,2,1,0:T(4,128)(2,1)} async-done(((bf16[32,1,1,3,4096]{4,3,2,1,0:T(4,128)(2,1)}), bf16[32,1,1,3,4096]{4,3,2,1,0:T(4,128)(2,1)}, u32[]{:S(2)}, u32[]{:S(2)}) %all-to-all-start.1) | async-done | bytes 786464 | tf_op jit(solution)/shard_map/all_to_all | solution.py:33
  267.9 4.7 all-to-all-start.2
  272.6 10.2 %all-gather.5.cloned.1.call-start = ((), (), s32[]{:S(2)}) async-start(), calls=%async_computation.10 | async-start | bytes 7864320 | tf_op jit(solution)/shard_map/all_gather | solution.py:51
  282.8 0.2 fusion.68
  283.0 6.4 %all-to-all-done.2 = bf16[32,1,1,3,4096]{4,3,2,1,0:T(4,128)(2,1)} async-done(((bf16[32,1,1,3,4096]{4,3,2,1,0:T(4,128)(2,1)}), bf16[32,1,1,3,4096]{4,3,2,1,0:T(4,128)(2,1)}, u32[]{:S(2)}, u32[]{:S(2)}) %all-to-all-start.2) | async-done | bytes 786464 | tf_op jit(solution)/shard_map/all_to_all | solution.py:33
  289.4 3.9 pad_maximum_fusion
  293.3 3.7 reshape_reshape.6
  297.0 2.0 fusion.50
  299.0 0.1 copy-done.6
  299.1 2.1 fusion.42
  301.3 0.2 fusion.59
  301.6 0.7 fusion.46
  302.3 1.8 fusion.31
  304.1 3.5 reshape.161
  307.6 31.9 %all_to_all.45 = bf16[32,1,6,4096]{3,2,1,0:T(8,128)(2,1)} all-to-all(bf16[32,1,6,4096]{3,2,1,0:T(8,128)(2,1)} %bitcast.96), channel_id=1, replica_groups=mesh['node'=32,'local'=4] {'node'}, dimensions={0} | all-to-all | bytes 3145728 | tf_op jit(solution)/shard_map/all_to_all | solution.py:50
  339.5 3.7 all_to_all.35
  343.2 0.0 reduce-scatter.5.cloned.1.call-start
  343.2 47.0 %all-gather.5.cloned.1.call-done = bf16[1,1,768,4096]{3,2,1,0:T(8,128)(2,1)} async-done(((bf16[1,1,192,4096]{3,2,1,0:T(8,128)(2,1)}), bf16[1,1,768,4096]{3,2,1,0:T(8,128)(2,1)}) %all-gather.5.cloned.1.call-update) | async-done | bytes 6291472 | tf_op jit(solution)/shard_map/all_gather | solution.py:51
  390.3 7.3 %multiply_convert_fusion = (bf16[768,384]{1,0:T(8,128)(2,1)S(1)}, bf16[768,384]{1,0:T(8,128)(2,1)S(1)}) fusion(f32[768,384]{1,0:T(8,128)} %copy-done.20, f32[768,384]{1,0:T(8,128)} %get-tuple-element.27, bf16[1,384,4096]{2,1,0:T(8,128)(2,1)S(1)} %copy-done, bf16[1,1,768,4096]{3,2,1,0:T(8,128)(2,1)} %all-gather.5.cloned.1.call-done), kind=kOutput, calls=%fused_computation.44 | convolution fusion | flops 2419752960 | bytes 12976128 | tf_op jit(solution)/shard_map/erd,efd->erf/dot_general | solution.py:103
  397.6 3.5 fusion.37
  401.1 6.5 %add_bitcast_fusion = f32[1,1,768,4096]{3,2,1,0:T(8,128)} fusion(f32[768,4096]{1,0:T(8,128)S(1)} %fusion.37, bf16[768,384]{1,0:T(8,128)(2,1)S(1)} %get-tuple-element.14, bf16[1,4096,384]{2,1,0:T(8,128)(2,1)S(1)} %copy-done.11), kind=kOutput, calls=%fused_computation | convolution fusion | flops 2419064832 | bytes 28901376 | tf_op jit(solution)/shard_map/erf,edf->erd/dot_general | solution.py:110
  407.6 0.1 select_reduce_fusion
  407.8 1.4 copy-done.3
  409.2 3.0 add_convert_fusion
  412.2 100.9 %reduce-scatter.5.cloned.1.call-done = f32[1,1,192,4096]{3,2,1,0:T(8,128)} async-done(((f32[1,1,768,4096]{3,2,1,0:T(8,128)}), f32[1,1,192,4096]{3,2,1,0:T(8,128)}) %reduce-scatter.5.cloned.1.call-update) | async-done | bytes 3145744 | tf_op jit(solution)/shard_map/reduce_scatter | solution.py:56
  513.1 3.2 convert_element_type.74
  516.3 2.4 transpose_reshape.7
  518.7 2.5 slice_bitcast_fusion.1
  521.2 7.5 %all-to-all-start.4 = ((bf16[32,1,1,3,4096]{4,3,2,1,0:T(4,128)(2,1)}), bf16[32,1,1,3,4096]{4,3,2,1,0:T(4,128)(2,1)S(1)}, u32[]{:S(2)}, u32[]{:S(2)}) async-start(bf16[32,1,1,3,4096]{4,3,2,1,0:T(4,128)(2,1)} %get-tuple-element.16), calls=%async_computation.6 | async-start | bytes 2097152 | tf_op jit(solution)/shard_map/all_to_all | solution.py:33
  528.7 0.8 fusion.56
  529.5 7.9 %fusion.24 = bf16[1,4096,384]{2,1,0:T(8,128)(2,1)} fusion(bf16[768,384]{1,0:T(8,128)(2,1)S(1)} %copy-done.15, bf16[1,1,768,4096]{3,2,1,0:T(8,128)(2,1)} %all-gather.3.cloned.1.call-done), kind=kOutput, calls=%fused_computation.20 | convolution fusion | flops 2417491968 | bytes 10027008 | tf_op jit(solution)/shard_map/erd,erf->edf/dot_general | solution.py:115
  537.5 8.9 %all-to-all-done.4 = bf16[32,1,1,3,4096]{4,3,2,1,0:T(4,128)(2,1)S(1)} async-done(((bf16[32,1,1,3,4096]{4,3,2,1,0:T(4,128)(2,1)}), bf16[32,1,1,3,4096]{4,3,2,1,0:T(4,128)(2,1)S(1)}, u32[]{:S(2)}, u32[]{:S(2)}) %all-to-all-start.4) | async-done | bytes 786464 | tf_op jit(solution)/shard_map/all_to_all | solution.py:33
  546.4 4.7 all-to-all-start.5
  551.1 7.2 %fusion.21 = bf16[1,384,4096]{2,1,0:T(8,128)(2,1)} fusion(bf16[768,384]{1,0:T(8,128)(2,1)S(1)} %copy-done.9, bf16[1,1,768,4096]{3,2,1,0:T(8,128)(2,1)} %all-gather.5.cloned.1.call-done), kind=kOutput, calls=%fused_computation.19 | convolution fusion | flops 2417491968 | bytes 10027008 | tf_op jit(solution)/shard_map/erf,erd->efd/dot_general | solution.py:118
  558.3 7.9 %fusion.27 = bf16[1,4096,384]{2,1,0:T(8,128)(2,1)} fusion(bf16[768,384]{1,0:T(8,128)(2,1)S(1)} %copy-done.17, bf16[1,1,768,4096]{3,2,1,0:T(8,128)(2,1)} %all-gather.3.cloned.1.call-done), kind=kOutput, calls=%fused_computation.21 | convolution fusion | flops 2417491968 | bytes 10027008 | tf_op jit(solution)/shard_map/erd,erf->edf/dot_general | solution.py:112
  566.2 1.7 all-to-all-done.5
  567.9 2.3 pad_maximum_fusion.1
  570.2 1.4 reshape_reshape.7
  571.6 2.0 fusion.51
  573.7 1.5 fusion.32
  (60 shorter events, 0.4 us)
Async XLA Ops:
  7.2 112.2 %copy-start = (bf16[1,384,4096]{2,1,0:T(8,128)(2,1)S(1)}, bf16[1,384,4096]{2,1,0:T(8,128)(2,1)}, u32[]{:S(2)}) copy-start(bf16[1,384,4096]{2,1,0:T(8,128)(2,1)} %param.15) | copy-start | bytes 9437188
  7.2 100.2 %all-gather.3.cloned.1.call-start = ((), (), s32[]{:S(2)}) async-start(), calls=%async_computation.8 | async-start | bytes 7864320 | tf_op jit(solution)/shard_map/all_gather | solution.py:51
  9.9 1.9 copy-start.7
  58.6 172.6 %reduce-scatter.3.cloned.1.call-start = ((), (), s32[]{:S(2)}) async-start(), calls=%async_computation.9 | async-start | bytes 15728640 | tf_op jit(solution)/shard_map/reduce_scatter | solution.py:56
  107.4 6.6 %copy-start.10 = (bf16[1,4096,384]{2,1,0:T(8,128)(2,1)S(1)}, bf16[1,4096,384]{2,1,0:T(8,128)(2,1)}, u32[]{:S(2)}) copy-start(bf16[1,4096,384]{2,1,0:T(8,128)(2,1)} %param.14) | copy-start | bytes 9437188
  107.4 6.6 %copy-start.19 = (bf16[1,1,768,4096]{3,2,1,0:T(8,128)(2,1)S(1)}, bf16[1,1,768,4096]{3,2,1,0:T(8,128)(2,1)}, u32[]{:S(2)}) copy-start(bf16[1,1,768,4096]{3,2,1,0:T(8,128)(2,1)} %all-gather.3.cloned.1.call-done) | copy-start | bytes 18874372
  114.0 4.5 copy-start.20
  118.5 0.8 copy-start.8
  242.6 7.5 %copy-start.13 = (f32[128,128]{1,0:T(8,128)S(1)}, f32[128,128]{1,0:T(8,128)}, u32[]{:S(2)}) copy-start(f32[128,128]{1,0:T(8,128)} %param.10) | copy-start | bytes 196612
  242.6 25.3 %all-to-all-start.1 = ((bf16[32,1,1,3,4096]{4,3,2,1,0:T(4,128)(2,1)}), bf16[32,1,1,3,4096]{4,3,2,1,0:T(4,128)(2,1)}, u32[]{:S(2)}, u32[]{:S(2)}) async-start(bf16[32,1,1,3,4096]{4,3,2,1,0:T(4,128)(2,1)} %get-tuple-element.18), calls=%async_computation.2 | async-start | bytes 2097152 | tf_op jit(solution)/shard_map/all_to_all | solution.py:33
  267.9 21.5 %all-to-all-start.2 = ((bf16[32,1,1,3,4096]{4,3,2,1,0:T(4,128)(2,1)}), bf16[32,1,1,3,4096]{4,3,2,1,0:T(4,128)(2,1)}, u32[]{:S(2)}, u32[]{:S(2)}) async-start(bf16[32,1,1,3,4096]{4,3,2,1,0:T(4,128)(2,1)} %get-tuple-element.19), calls=%async_computation.3 | async-start | bytes 2097152 | tf_op jit(solution)/shard_map/all_to_all | solution.py:33
  272.6 117.7 %all-gather.5.cloned.1.call-start = ((), (), s32[]{:S(2)}) async-start(), calls=%async_computation.10 | async-start | bytes 7864320 | tf_op jit(solution)/shard_map/all_gather | solution.py:51
  297.0 2.1 copy-start.5
  297.0 2.2 copy-start.6
  299.1 2.2 copy-start.2
  299.1 2.2 copy-start.18
  343.2 169.9 %reduce-scatter.5.cloned.1.call-start = ((), (), s32[]{:S(2)}) async-start(), calls=%async_computation.11 | async-start | bytes 15728640 | tf_op jit(solution)/shard_map/reduce_scatter | solution.py:56
  390.3 7.3 %copy-start.12 = (bf16[1,4096,384]{2,1,0:T(8,128)(2,1)S(1)}, bf16[1,4096,384]{2,1,0:T(8,128)(2,1)}, u32[]{:S(2)}) copy-start(bf16[1,4096,384]{2,1,0:T(8,128)(2,1)} %param.13) | copy-start | bytes 9437188
  397.6 3.5 copy-start.16
  397.6 3.5 copy-start.14
  397.6 3.5 copy-start.11
  407.6 1.6 copy-start.3
  521.2 8.3 %copy-start.15 = (bf16[768,384]{1,0:T(8,128)(2,1)S(1)}, bf16[768,384]{1,0:T(8,128)(2,1)}, u32[]{:S(2)}) copy-start(bf16[768,384]{1,0:T(8,128)(2,1)} %copy-done.14) | copy-start | bytes 1769476
  521.2 25.2 %all-to-all-start.4 = ((bf16[32,1,1,3,4096]{4,3,2,1,0:T(4,128)(2,1)}), bf16[32,1,1,3,4096]{4,3,2,1,0:T(4,128)(2,1)S(1)}, u32[]{:S(2)}, u32[]{:S(2)}) async-start(bf16[32,1,1,3,4096]{4,3,2,1,0:T(4,128)(2,1)} %get-tuple-element.16), calls=%async_computation.6 | async-start | bytes 2097152 | tf_op jit(solution)/shard_map/all_to_all | solution.py:33
  537.5 13.6 %copy-start.9 = (bf16[768,384]{1,0:T(8,128)(2,1)S(1)}, bf16[768,384]{1,0:T(8,128)(2,1)}, u32[]{:S(2)}) copy-start(bf16[768,384]{1,0:T(8,128)(2,1)} %copy-done.8) | copy-start | bytes 1769476
  546.4 21.5 %all-to-all-start.5 = ((bf16[32,1,1,3,4096]{4,3,2,1,0:T(4,128)(2,1)}), bf16[32,1,1,3,4096]{4,3,2,1,0:T(4,128)(2,1)}, u32[]{:S(2)}, u32[]{:S(2)}) async-start(bf16[32,1,1,3,4096]{4,3,2,1,0:T(4,128)(2,1)} %get-tuple-element.17), calls=%async_computation.7 | async-start | bytes 2097152 | tf_op jit(solution)/shard_map/all_to_all | solution.py:33
  551.1 7.2 %copy-start.17 = (bf16[768,384]{1,0:T(8,128)(2,1)S(1)}, bf16[768,384]{1,0:T(8,128)(2,1)}, u32[]{:S(2)}) copy-start(bf16[768,384]{1,0:T(8,128)(2,1)} %copy-done.16) | copy-start | bytes 1769476
  571.6 2.1 copy-start.4
  571.6 3.5 copy-start.1
Sparse Core Ops, SparseCore 0:
  58.7 48.6 all-gather.2
  125.9 105.2 reduce-scatter.2
  343.3 46.9 all-gather.4
  407.7 105.3 reduce-scatter.4
where the time goes:
time: 591 us; the launch traced here: 582 us
  waiting for transfers between devices  337 us (57%)
  matrix products  71.5 us (12%)
  blocking collectives  69.8 us (12%)
  local copies, waits for them, and re-layouts  35.1 us (6%)
  starting transfers between devices  34.6 us (6%)
  other arithmetic  19.9 us (3%)
  between operations  14.5 us (2%)
    reduce_scatter x2, waiting for transfers between devices, collect(): lax.psum_scatter(partial_sums[None], 'local', scatter_dimension=2, tiled=...  206 us
    all_gather x2, waiting for transfers between devices, spread(): arrived = lax.all_gather(arrived, 'local', axis=2, tiled=True)  95.8 us
    all_to_all x2, blocking collectives, spread(): lax.all_to_all(buffer, 'node', split_axis=0, concat_axis=2, tiled=True)  69.8 us
    all_to_all x4, waiting for transfers between devices, exchange_in_pieces(): lax.all_to_all(piece, axis, split_axis=0, concat_axis=0, tiled=True)  34.5 us
    all_to_all x4, starting transfers between devices, exchange_in_pieces(): lax.all_to_all(piece, axis, split_axis=0, concat_axis=0, tiled=True)  24.3 us
  transfers between devices with their start and end apart: 8, of which 8 were waited for; matrix products, arithmetic and copies ran while one was open for 5% of the time, Pallas kernels for 0%

commit v1 on v0

--- a/solution.py
+++ b/solution.py
@@ -47,7 +47,10 @@
 
 
 def spread(buffer):
-    arrived = lax.all_to_all(buffer, "node", split_axis=0, concat_axis=2, tiled=True)
+    arrived = jnp.concatenate(
+        lax.all_to_all(jnp.stack(jnp.split(buffer, lax.axis_size("node"), axis=0)), "node", 0, 0),
+        axis=2,
+    )
     arrived = lax.all_gather(arrived, "local", axis=2, tiled=True)
     return arrived[0]
 

time: 591 us -> 582 us (0.985)
    all_to_all x2 -> x0, local copies, waits for them, and re-layouts: 7.32 us -> none  [spread(): lax.all_to_all(buffer, 'node', split_axis=0, concat_axis=2, tiled=True)]
where the time goes in v1:
time: 582 us; the launch traced here: 573 us
  waiting for transfers between devices  336 us (58%)
  matrix products  69.2 us (12%)
  blocking collectives  68.6 us (12%)
  starting transfers between devices  34.8 us (6%)
  local copies, waits for them, and re-layouts  29.3 us (5%)
  other arithmetic  19.9 us (3%)
  between operations  15 us (3%)
    reduce_scatter x2, waiting for transfers between devices, collect(): lax.psum_scatter(partial_sums[None], 'local', scatter_dimension=2, tiled=...  206 us
    all_gather x2, waiting for transfers between devices, spread(): arrived = lax.all_gather(arrived, 'local', axis=2, tiled=True)  95.8 us
    all_to_all x2, blocking collectives, spread(): lax.all_to_all(jnp.stack(jnp.split(buffer, lax.axis_size('node'), axis=0)...  68.6 us
    all_to_all x4, waiting for transfers between devices, exchange_in_pieces(): lax.all_to_all(piece, axis, split_axis=0, concat_axis=0, tiled=True)  34.3 us
    all_to_all x4, starting transfers between devices, exchange_in_pieces(): lax.all_to_all(piece, axis, split_axis=0, concat_axis=0, tiled=True)  24.3 us
  transfers between devices with their start and end apart: 8, of which 8 were waited for; matrix products, arithmetic and copies ran while one was open for 5% of the time, Pallas kernels for 0%

profile of v1, /device:TPU:0, one launch (start us, length us, event | category | flops | bytes accessed | tf_op | source)
XLA Modules:
  0.0 573.2 jit_solution(5687925408890282995)
XLA Ops:
  7.2 0.0 all-gather.3.cloned.1.call-start
  7.2 0.8 broadcast_compare_fusion
  8.0 0.8 broadcast_multiply_fusion
  8.8 0.7 broadcast_select_fusion
  9.5 0.1 copy.27
  9.6 0.2 reduce_window_sum.11
  9.8 0.1 copy.29
  9.9 1.9 fusion.53
  11.8 0.6 fusion.30
  13.2 37.7 %all_to_all.30 = bf16[32,1,1,6,4096]{4,3,2,1,0:T(8,128)(2,1)} all-to-all(bf16[32,1,1,6,4096]{4,3,2,1,0:T(8,128)(2,1)S(1)} %constant_dynamic-update-slice_fusion), channel_id=1, replica_groups=mesh['node'=32,'local'=4] {'node'}, dimensions={0} | all-to-all | bytes 3145728 | tf_op jit(solution)/shard_map/all_to_all | solution.py:51
  50.9 3.7 reshape.280
  54.6 0.0 all-gather.3.cloned.1.call-update
  54.6 0.0 reduce-scatter.3.cloned.1.call-start
  54.7 48.7 %all-gather.3.cloned.1.call-done = bf16[1,1,768,4096]{3,2,1,0:T(8,128)(2,1)} async-done(((bf16[1,1,192,4096]{3,2,1,0:T(8,128)(2,1)}), bf16[1,1,768,4096]{3,2,1,0:T(8,128)(2,1)}) %all-gather.3.cloned.1.call-update) | async-done | bytes 6291472 | tf_op jit(solution)/shard_map/all_gather | solution.py:54
  103.4 6.6 %fusion.10 = f32[768,384]{1,0:T(8,128)S(1)} fusion(bf16[1,1,768,4096]{3,2,1,0:T(8,128)(2,1)} %all-gather.3.cloned.1.call-done, bf16[1,4096,384]{2,1,0:T(8,128)(2,1)} %param.13), kind=kOutput, calls=%fused_computation.12 | convolution fusion | flops 2415919104 | bytes 10616832 | tf_op jit(solution)/shard_map/erd,edf->erf/dot_general | solution.py:98
  110.0 4.5 multiply_convert_fusion.2
  114.5 0.8 copy-done.8
  115.3 6.4 %convolution_bitcast_fusion = f32[1,1,768,4096]{3,2,1,0:T(8,128)} fusion(bf16[768,384]{1,0:T(8,128)(2,1)S(1)} %get-tuple-element.26, bf16[1,384,4096]{2,1,0:T(8,128)(2,1)S(1)} %copy-done), kind=kOutput, calls=%fused_computation.1 | convolution fusion | flops 2415919104 | bytes 16318464 | tf_op jit(solution)/shard_map/erf,efd->erd/dot_general | solution.py:103
  121.8 105.4 %reduce-scatter.3.cloned.1.call-done = f32[1,1,192,4096]{3,2,1,0:T(8,128)} async-done(((f32[1,1,768,4096]{3,2,1,0:T(8,128)}), f32[1,1,192,4096]{3,2,1,0:T(8,128)}) %reduce-scatter.3.cloned.1.call-update) | async-done | bytes 3145744 | tf_op jit(solution)/shard_map/reduce_scatter | solution.py:59
  227.2 3.2 convert_element_type.66
  230.4 3.5 transpose_reshape.6
  233.9 4.7 slice_bitcast_fusion.3
  238.6 7.5 %all-to-all-start.1 = ((bf16[32,1,1,3,4096]{4,3,2,1,0:T(4,128)(2,1)}), bf16[32,1,1,3,4096]{4,3,2,1,0:T(4,128)(2,1)}, u32[]{:S(2)}, u32[]{:S(2)}) async-start(bf16[32,1,1,3,4096]{4,3,2,1,0:T(4,128)(2,1)} %get-tuple-element.18), calls=%async_computation.2 | async-start | bytes 2097152 | tf_op jit(solution)/shard_map/all_to_all | solution.py:33
  246.1 0.1 reduce_max.18
  246.2 0.2 select_reduce_fusion.1
  246.4 17.5 %all-to-all-done.1 = bf16[32,1,1,3,4096]{4,3,2,1,0:T(4,128)(2,1)} async-done(((bf16[32,1,1,3,4096]{4,3,2,1,0:T(4,128)(2,1)}), bf16[32,1,1,3,4096]{4,3,2,1,0:T(4,128)(2,1)}, u32[]{:S(2)}, u32[]{:S(2)}) %all-to-all-start.1) | async-done | bytes 786464 | tf_op jit(solution)/shard_map/all_to_all | solution.py:33
  263.9 4.7 all-to-all-start.2
  268.6 10.4 %all-gather.5.cloned.1.call-start = ((), (), s32[]{:S(2)}) async-start(), calls=%async_computation.10 | async-start | bytes 7864320 | tf_op jit(solution)/shard_map/all_gather | solution.py:54
  279.0 0.2 fusion.68
  279.2 6.2 %all-to-all-done.2 = bf16[32,1,1,3,4096]{4,3,2,1,0:T(4,128)(2,1)} async-done(((bf16[32,1,1,3,4096]{4,3,2,1,0:T(4,128)(2,1)}), bf16[32,1,1,3,4096]{4,3,2,1,0:T(4,128)(2,1)}, u32[]{:S(2)}, u32[]{:S(2)}) %all-to-all-start.2) | async-done | bytes 786464 | tf_op jit(solution)/shard_map/all_to_all | solution.py:33
  285.4 3.9 pad_maximum_fusion
  289.3 3.7 reshape_reshape.6
  293.0 2.0 fusion.50
  295.0 0.1 copy-done.6
  295.1 2.1 fusion.42
  297.3 0.2 fusion.59
  297.6 0.7 fusion.46
  298.3 0.7 fusion.31
  299.8 30.9 %all_to_all.31 = bf16[32,1,1,6,4096]{4,3,2,1,0:T(8,128)(2,1)} all-to-all(bf16[32,1,1,6,4096]{4,3,2,1,0:T(8,128)(2,1)S(1)} %constant_dynamic-update-slice_fusion.32), channel_id=1, replica_groups=mesh['node'=32,'local'=4] {'node'}, dimensions={0} | all-to-all | bytes 3145728 | tf_op jit(solution)/shard_map/all_to_all | solution.py:51
  330.6 3.7 reshape.285
  334.3 0.0 reduce-scatter.5.cloned.1.call-start
  334.4 47.0 %all-gather.5.cloned.1.call-done = bf16[1,1,768,4096]{3,2,1,0:T(8,128)(2,1)} async-done(((bf16[1,1,192,4096]{3,2,1,0:T(8,128)(2,1)}), bf16[1,1,768,4096]{3,2,1,0:T(8,128)(2,1)}) %all-gather.5.cloned.1.call-update) | async-done | bytes 6291472 | tf_op jit(solution)/shard_map/all_gather | solution.py:54
  381.4 7.3 %multiply_convert_fusion = (bf16[768,384]{1,0:T(8,128)(2,1)S(1)}, bf16[768,384]{1,0:T(8,128)(2,1)S(1)}) fusion(f32[768,384]{1,0:T(8,128)} %copy-done.20, f32[768,384]{1,0:T(8,128)} %get-tuple-element.27, bf16[1,384,4096]{2,1,0:T(8,128)(2,1)S(1)} %copy-done, bf16[1,1,768,4096]{3,2,1,0:T(8,128)(2,1)} %all-gather.5.cloned.1.call-done), kind=kOutput, calls=%fused_computation.44 | convolution fusion | flops 2419752960 | bytes 12976128 | tf_op jit(solution)/shard_map/erd,efd->erf/dot_general | solution.py:106
  388.7 3.5 fusion.37
  392.2 6.5 %add_bitcast_fusion = f32[1,1,768,4096]{3,2,1,0:T(8,128)} fusion(f32[768,4096]{1,0:T(8,128)S(1)} %fusion.37, bf16[768,384]{1,0:T(8,128)(2,1)S(1)} %get-tuple-element.14, bf16[1,4096,384]{2,1,0:T(8,128)(2,1)S(1)} %copy-done.11), kind=kOutput, calls=%fused_computation | convolution fusion | flops 2419064832 | bytes 28901376 | tf_op jit(solution)/shard_map/erf,edf->erd/dot_general | solution.py:113
  398.7 0.1 select_reduce_fusion
  398.9 1.4 copy-done.3
  400.3 3.0 add_convert_fusion
  403.3 100.9 %reduce-scatter.5.cloned.1.call-done = f32[1,1,192,4096]{3,2,1,0:T(8,128)} async-done(((f32[1,1,768,4096]{3,2,1,0:T(8,128)}), f32[1,1,192,4096]{3,2,1,0:T(8,128)}) %reduce-scatter.5.cloned.1.call-update) | async-done | bytes 3145744 | tf_op jit(solution)/shard_map/reduce_scatter | solution.py:59
  504.2 3.2 convert_element_type.74
  507.4 2.4 transpose_reshape.7
  509.9 2.5 slice_bitcast_fusion.1
  512.4 7.5 %all-to-all-start.4 = ((bf16[32,1,1,3,4096]{4,3,2,1,0:T(4,128)(2,1)}), bf16[32,1,1,3,4096]{4,3,2,1,0:T(4,128)(2,1)S(1)}, u32[]{:S(2)}, u32[]{:S(2)}) async-start(bf16[32,1,1,3,4096]{4,3,2,1,0:T(4,128)(2,1)} %get-tuple-element.16), calls=%async_computation.6 | async-start | bytes 2097152 | tf_op jit(solution)/shard_map/all_to_all | solution.py:33
  519.9 0.8 fusion.56
  520.7 7.9 %fusion.24 = bf16[1,4096,384]{2,1,0:T(8,128)(2,1)} fusion(bf16[768,384]{1,0:T(8,128)(2,1)S(1)} %copy-done.15, bf16[1,1,768,4096]{3,2,1,0:T(8,128)(2,1)} %all-gather.3.cloned.1.call-done), kind=kOutput, calls=%fused_computation.20 | convolution fusion | flops 2417491968 | bytes 10027008 | tf_op jit(solution)/shard_map/erd,erf->edf/dot_general | solution.py:118
  528.6 8.9 %all-to-all-done.4 = bf16[32,1,1,3,4096]{4,3,2,1,0:T(4,128)(2,1)S(1)} async-done(((bf16[32,1,1,3,4096]{4,3,2,1,0:T(4,128)(2,1)}), bf16[32,1,1,3,4096]{4,3,2,1,0:T(4,128)(2,1)S(1)}, u32[]{:S(2)}, u32[]{:S(2)}) %all-to-all-start.4) | async-done | bytes 786464 | tf_op jit(solution)/shard_map/all_to_all | solution.py:33
  537.5 4.7 all-to-all-start.5
  542.2 7.2 %fusion.21 = bf16[1,384,4096]{2,1,0:T(8,128)(2,1)} fusion(bf16[768,384]{1,0:T(8,128)(2,1)S(1)} %copy-done.9, bf16[1,1,768,4096]{3,2,1,0:T(8,128)(2,1)} %all-gather.5.cloned.1.call-done), kind=kOutput, calls=%fused_computation.19 | convolution fusion | flops 2417491968 | bytes 10027008 | tf_op jit(solution)/shard_map/erf,erd->efd/dot_general | solution.py:121
  549.4 7.9 %fusion.27 = bf16[1,4096,384]{2,1,0:T(8,128)(2,1)} fusion(bf16[768,384]{1,0:T(8,128)(2,1)S(1)} %copy-done.17, bf16[1,1,768,4096]{3,2,1,0:T(8,128)(2,1)} %all-gather.3.cloned.1.call-done), kind=kOutput, calls=%fused_computation.21 | convolution fusion | flops 2417491968 | bytes 10027008 | tf_op jit(solution)/shard_map/erd,erf->edf/dot_general | solution.py:115
  557.3 1.7 all-to-all-done.5
  559.0 2.3 pad_maximum_fusion.1
  561.3 1.4 reshape_reshape.7
  562.7 2.0 fusion.51
  564.8 1.5 fusion.32
  (122 shorter events, 1.6 us)
Async XLA Ops:
  7.2 108.2 %copy-start = (bf16[1,384,4096]{2,1,0:T(8,128)(2,1)S(1)}, bf16[1,384,4096]{2,1,0:T(8,128)(2,1)}, u32[]{:S(2)}) copy-start(bf16[1,384,4096]{2,1,0:T(8,128)(2,1)} %param.15) | copy-start | bytes 9437188
  7.2 96.2 %all-gather.3.cloned.1.call-start = ((), (), s32[]{:S(2)}) async-start(), calls=%async_computation.8 | async-start | bytes 7864320 | tf_op jit(solution)/shard_map/all_gather | solution.py:54
  9.9 1.9 copy-start.7
  54.6 172.6 %reduce-scatter.3.cloned.1.call-start = ((), (), s32[]{:S(2)}) async-start(), calls=%async_computation.9 | async-start | bytes 15728640 | tf_op jit(solution)/shard_map/reduce_scatter | solution.py:59
  103.4 6.6 %copy-start.10 = (bf16[1,4096,384]{2,1,0:T(8,128)(2,1)S(1)}, bf16[1,4096,384]{2,1,0:T(8,128)(2,1)}, u32[]{:S(2)}) copy-start(bf16[1,4096,384]{2,1,0:T(8,128)(2,1)} %param.14) | copy-start | bytes 9437188
  103.4 6.6 %copy-start.19 = (bf16[1,1,768,4096]{3,2,1,0:T(8,128)(2,1)S(1)}, bf16[1,1,768,4096]{3,2,1,0:T(8,128)(2,1)}, u32[]{:S(2)}) copy-start(bf16[1,1,768,4096]{3,2,1,0:T(8,128)(2,1)} %all-gather.3.cloned.1.call-done) | copy-start | bytes 18874372
  110.0 4.5 copy-start.20
  114.5 0.8 copy-start.8
  238.6 7.5 %copy-start.13 = (f32[128,128]{1,0:T(8,128)S(1)}, f32[128,128]{1,0:T(8,128)}, u32[]{:S(2)}) copy-start(f32[128,128]{1,0:T(8,128)} %param.10) | copy-start | bytes 196612
  238.6 25.3 %all-to-all-start.1 = ((bf16[32,1,1,3,4096]{4,3,2,1,0:T(4,128)(2,1)}), bf16[32,1,1,3,4096]{4,3,2,1,0:T(4,128)(2,1)}, u32[]{:S(2)}, u32[]{:S(2)}) async-start(bf16[32,1,1,3,4096]{4,3,2,1,0:T(4,128)(2,1)} %get-tuple-element.18), calls=%async_computation.2 | async-start | bytes 2097152 | tf_op jit(solution)/shard_map/all_to_all | solution.py:33
  263.9 21.5 %all-to-all-start.2 = ((bf16[32,1,1,3,4096]{4,3,2,1,0:T(4,128)(2,1)}), bf16[32,1,1,3,4096]{4,3,2,1,0:T(4,128)(2,1)}, u32[]{:S(2)}, u32[]{:S(2)}) async-start(bf16[32,1,1,3,4096]{4,3,2,1,0:T(4,128)(2,1)} %get-tuple-element.19), calls=%async_computation.3 | async-start | bytes 2097152 | tf_op jit(solution)/shard_map/all_to_all | solution.py:33
  268.6 112.8 %all-gather.5.cloned.1.call-start = ((), (), s32[]{:S(2)}) async-start(), calls=%async_computation.10 | async-start | bytes 7864320 | tf_op jit(solution)/shard_map/all_gather | solution.py:54
  293.0 2.1 copy-start.5
  293.0 2.2 copy-start.6
  295.1 2.1 copy-start.2
  295.1 2.2 copy-start.18
  334.3 169.9 %reduce-scatter.5.cloned.1.call-start = ((), (), s32[]{:S(2)}) async-start(), calls=%async_computation.11 | async-start | bytes 15728640 | tf_op jit(solution)/shard_map/reduce_scatter | solution.py:59
  381.4 7.3 %copy-start.12 = (bf16[1,4096,384]{2,1,0:T(8,128)(2,1)S(1)}, bf16[1,4096,384]{2,1,0:T(8,128)(2,1)}, u32[]{:S(2)}) copy-start(bf16[1,4096,384]{2,1,0:T(8,128)(2,1)} %param.13) | copy-start | bytes 9437188
  388.7 3.5 copy-start.16
  388.7 3.5 copy-start.14
  388.7 3.5 copy-start.11
  398.7 1.6 copy-start.3
  512.4 8.3 %copy-start.15 = (bf16[768,384]{1,0:T(8,128)(2,1)S(1)}, bf16[768,384]{1,0:T(8,128)(2,1)}, u32[]{:S(2)}) copy-start(bf16[768,384]{1,0:T(8,128)(2,1)} %copy-done.14) | copy-start | bytes 1769476
  512.4 25.2 %all-to-all-start.4 = ((bf16[32,1,1,3,4096]{4,3,2,1,0:T(4,128)(2,1)}), bf16[32,1,1,3,4096]{4,3,2,1,0:T(4,128)(2,1)S(1)}, u32[]{:S(2)}, u32[]{:S(2)}) async-start(bf16[32,1,1,3,4096]{4,3,2,1,0:T(4,128)(2,1)} %get-tuple-element.16), calls=%async_computation.6 | async-start | bytes 2097152 | tf_op jit(solution)/shard_map/all_to_all | solution.py:33
  528.6 13.6 %copy-start.9 = (bf16[768,384]{1,0:T(8,128)(2,1)S(1)}, bf16[768,384]{1,0:T(8,128)(2,1)}, u32[]{:S(2)}) copy-start(bf16[768,384]{1,0:T(8,128)(2,1)} %copy-done.8) | copy-start | bytes 1769476
  537.5 21.5 %all-to-all-start.5 = ((bf16[32,1,1,3,4096]{4,3,2,1,0:T(4,128)(2,1)}), bf16[32,1,1,3,4096]{4,3,2,1,0:T(4,128)(2,1)}, u32[]{:S(2)}, u32[]{:S(2)}) async-start(bf16[32,1,1,3,4096]{4,3,2,1,0:T(4,128)(2,1)} %get-tuple-element.17), calls=%async_computation.7 | async-start | bytes 2097152 | tf_op jit(solution)/shard_map/all_to_all | solution.py:33
  542.2 7.2 %copy-start.17 = (bf16[768,384]{1,0:T(8,128)(2,1)S(1)}, bf16[768,384]{1,0:T(8,128)(2,1)}, u32[]{:S(2)}) copy-start(bf16[768,384]{1,0:T(8,128)(2,1)} %copy-done.16) | copy-start | bytes 1769476
  562.7 2.1 copy-start.4
  562.7 3.5 copy-start.1
Sparse Core Ops, SparseCore 0:
  54.7 48.6 all-gather.2
  121.9 105.2 reduce-scatter.2
  334.4 46.9 all-gather.4
  398.9 105.3 reduce-scatter.4
